TPU v7x, 32 devices: a whole 2x2x4 slice. The times are simulated.
32 devices in a mesh: grp: 2 (over y), lat: 4 (over z), lon: 4 (over x, core).
Axes of the slice: x: 2, y: 2, z: 4, core: 2. Of those that a mesh axis runs over, the one named last changes fastest.
Arguments:
- features: bfloat16 [64, 512, 256], P(('grp', 'lat'), 'lon'), parts along dimension 0, may hold values from -6 to 6
- cotangent: bfloat16 [64, 512, 256], P(('grp', 'lat'), 'lon'), parts along dimension 0, may hold values from -6 to 6
- weights: bfloat16 [8, 256, 256], replicated, may hold values from -0.375 to 0.375
- coef_table: float32 [32, 8], replicated, may hold values from 0.05 to 4.5
- lat_index: int32 [32], P('lat'), may hold values from 0 to 31
- dir_ids: int32 [8], replicated, may hold values from 0 to 7, each once
Outputs:
- grad_features: bfloat16 [64, 512, 256], P(('grp', 'lat'), 'lon'), parts along dimension 0
- grad_weights: float32 [4096, 256], P(('grp', 'lat', 'lon')), parts along dimension 0
- grad_table: float32 [64, 8], P('grp'), parts along dimension 0
There are 2 independent parts, one for each index of `grp`. A program takes and returns all parts, laid end to end along the dimension named above; an argument that names none is the same for every part. Nothing has to cross between parts.
Inputs may be any that keep to these rules, and one draw needn't show every extreme that they name: `dir_ids`: each of the 8 directions belongs to exactly one expert.
All inputs are finite; a program needn't handle non-finite values.
Results may differ from a plain program's by a relative error of at most 0.0047.
Values may be sent and summed in bfloat16 or wider, within the bound.
A program may use at most 64 MiB of HBM per device.

v0:
```python
import jax
import jax.numpy as jnp
from jax import lax
from jax.sharding import PartitionSpec as P

STEP_PAIRS = ((-1, -1), (-1, 0), (-1, 1), (0, -1), (0, 1), (1, -1), (1, 0), (1, 1))
clip_norm = 512.0


def with_halo(block, sides, width):
    for axis, dim in sides:
        count = lax.axis_size(axis)
        forward = [(i, i + 1) for i in range(count - 1)]
        forward.append((count - 1, 0))
        backward = [(target, source) for source, target in forward]
        low = lax.ppermute(
            lax.slice_in_dim(block, block.shape[dim] - width, None, axis=dim), axis, forward
        )
        high = lax.ppermute(lax.slice_in_dim(block, 0, width, axis=dim), axis, backward)
        block = jnp.concatenate([low, block, high], axis=dim)
    return block


def body(features, cotangent, weights, coef_table, lat_index, dir_ids):
    lat_rows, lon_cols, latent = features.shape
    experts = weights.shape[0]
    global_rows = coef_table.shape[0]
    lat_size = lax.axis_size("lat")
    lat_pos = lax.axis_index("lat")
    keep_top = (lat_pos > 0).astype(jnp.float32)
    keep_bottom = (lat_pos < lat_size - 1).astype(jnp.float32)
    padded = with_halo(features, (("lat", 0), ("lon", 1)), 1)
    padded = jnp.concatenate(
        [
            padded[:1] * keep_top.astype(jnp.bfloat16),
            padded[1:-1],
            padded[-1:] * keep_bottom.astype(jnp.bfloat16),
        ],
        axis=0,
    )
    shifted = jnp.stack(
        [
            padded[1 + lat_step : 1 + lat_step + lat_rows, 1 + lon_step : 1 + lon_step + lon_cols]
            for lat_step, lon_step in STEP_PAIRS
        ]
    )
    neighbours = jnp.take(shifted, dir_ids, axis=0).reshape(experts, lat_rows * lon_cols, latent)
    preact = jnp.einsum("epc,ecd->epd", neighbours, weights, preferred_element_type=jnp.float32)
    logistic = jax.nn.sigmoid(preact)
    activated = (preact * logistic).reshape(experts, lat_rows, lon_cols, latent)
    derivative = (logistic * (1.0 + preact * (1.0 - logistic))).reshape(
        experts, lat_rows, lon_cols, latent
    )
    picker = (lat_index[:, None] == jnp.arange(global_rows, dtype=jnp.int32)[None, :]).astype(
        jnp.float32
    )
    row_coef = jnp.dot(picker, coef_table, precision=lax.Precision.HIGHEST)
    grad32 = cotangent.astype(jnp.float32)
    row_sums = jnp.sum(grad32[None] * activated, axis=(2, 3))
    table_part = jnp.dot(picker.T, row_sums.T, precision=lax.Precision.HIGHEST)
    pre_grad = (grad32[None] * row_coef.T[:, :, None, None] * derivative).astype(jnp.bfloat16)
    pre_grad = pre_grad.reshape(experts, lat_rows * lon_cols, latent)
    weight_part = jnp.einsum(
        "epc,epd->ecd", neighbours, pre_grad, preferred_element_type=jnp.float32
    ).reshape(experts * latent, latent)
    returned = jnp.einsum(
        "epd,ecd->epc", pre_grad, weights, preferred_element_type=jnp.float32
    ).reshape(experts, lat_rows, lon_cols, latent)
    inverse = jnp.argsort(dir_ids)
    by_direction = jnp.take(returned, inverse, axis=0)
    spread = jnp.zeros((lat_rows + 2, lon_cols + 2, latent), jnp.float32)
    for index, (lat_step, lon_step) in enumerate(STEP_PAIRS):
        spread = spread + jnp.pad(
            by_direction[index],
            ((1 + lat_step, 1 - lat_step), (1 + lon_step, 1 - lon_step), (0, 0)),
        )
    rimmed = with_halo(spread, (("lat", 0), ("lon", 1)), 1)
    folded = rimmed[:, 2 : lon_cols + 2]
    folded = folded.at[:, 0].add(rimmed[:, 0]).at[:, lon_cols - 1].add(rimmed[:, lon_cols + 3])
    interior = folded[2 : lat_rows + 2]
    interior = (
        interior.at[0]
        .add(folded[0] * keep_top)
        .at[lat_rows - 1]
        .add(folded[lat_rows + 3] * keep_bottom)
    )
    grad_features = (grad32 + interior).astype(jnp.bfloat16)
    table_grad = lax.psum(table_part, ("lat", "lon"))
    weight_shard = lax.psum_scatter(weight_part, ("lat", "lon"), scatter_dimension=0, tiled=True)
    shard_squares = lax.psum(jnp.sum(weight_shard * weight_shard), ("lat", "lon"))
    squares = shard_squares + jnp.sum(table_grad * table_grad)
    factor = jnp.minimum(1.0, clip_norm / jnp.sqrt(squares + 1e-06))
    return (grad_features, factor * weight_shard, factor * table_grad)


def solution(mesh):
    in_specs = (
        P(("grp", "lat"), "lon", None),
        P(("grp", "lat"), "lon", None),
        P(),
        P(),
        P("lat"),
        P(),
    )
    out_specs = (P(("grp", "lat"), "lon", None), P(("grp", "lat", "lon"), None), P("grp", None))
    return jax.shard_map(body, mesh=mesh, in_specs=in_specs, out_specs=out_specs, check_vma=False)
```

profile of v0, /device:TPU:0, one launch (start us, length us, event | category | flops | bytes accessed | tf_op | source)
XLA Modules:
  0.0 159.0 jit_solution(13156924044293081186)
XLA Ops:
  7.2 1.0 fusion.33
  8.2 5.1 %collective-permute-start.1 = (bf16[1,128,256]{2,1,0:T(8,128)(2,1)S(1)}, bf16[1,128,256]{2,1,0:T(8,128)(2,1)S(1)}, u32[]{:S(2)}, u32[]{:S(2)}) collective-permute-start(bf16[1,128,256]{2,1,0:T(8,128)(2,1)S(1)} %get-tuple-element.73), channel_id=1, source_target_pairs={{4,0},{8,4},{12,8},{0,12},{5,1},{9,5},{13,9},{1,13},{6,2},{10,6},{... | collective-permute-start | bytes 196616 | tf_op jit(solution)/shard_map/ppermute | solution.py:19
  13.3 0.7 compare_select_fusion
  14.0 1.6 %sort.17 = (s32[8]{0:T(128)}, s32[8]{0:T(128)S(1)}) sort(s32[8]{0:T(128)} %param.19, s32[8]{0:T(128)S(1)} %iota.8), dimensions={0}, to_apply=%region_0.1 | sort | flops 24 | bytes 128 | tf_op jit(solution)/shard_map/jit(argsort)/sort | solution.py:69
  15.6 0.7 compare_and_fusion
  16.2 0.9 convolution_bitcast_fusion
  17.2 2.1 %collective-permute-done = bf16[1,128,256]{2,1,0:T(8,128)(2,1)S(1)} collective-permute-done((bf16[1,128,256]{2,1,0:T(8,128)(2,1)S(1)}, bf16[1,128,256]{2,1,0:T(8,128)(2,1)S(1)}, u32[]{:S(2)}, u32[]{:S(2)}) %collective-permute-start) | collective-permute-done | bytes 65568 | tf_op jit(solution)/shard_map/ppermute | solution.py:16
  19.4 1.1 constant_dynamic-update-slice_fusion.1
  20.6 1.7 %collective-permute-start.3 = (bf16[10,1,256]{2,1,0:T(2,128)(2,1)S(1)}, bf16[10,1,256]{2,1,0:T(2,128)(2,1)S(1)}, u32[]{:S(2)}, u32[]{:S(2)}) collective-permute-start(bf16[10,1,256]{2,1,0:T(2,128)(2,1)S(1)} %get-tuple-element.72), channel_id=1, source_target_pairs={{1,0},{2,1},{3,2},{0,3},{5,4},{6,5},{7,6},{4,7},{9,8},{10,9},{11,1... | collective-permute-start | bytes 15368 | tf_op jit(solution)/shard_map/ppermute | solution.py:19
  22.3 1.2 copy.15
  23.6 0.1 collective-permute-done.2
  23.7 0.2 pad_maximum_fusion.1
  24.0 0.8 fusion.13
  24.8 0.9 fusion.10
  25.8 0.9 fusion.21
  26.7 0.9 fusion.19
  27.6 0.9 fusion.17
  28.6 0.9 fusion.7
  29.4 0.9 fusion.4
  30.4 0.9 fusion.15
  31.3 4.9 %gather_fusion = bf16[8,8,128,256]{3,2,1,0:T(8,128)(2,1)} fusion(bf16[8,8,128,256]{3,2,1,0:T(8,128)(2,1)} %fusion.15, s32[1024]{0:T(1024)S(1)} %pad_clamp_fusion.1), kind=kCustom, calls=%fused_computation | custom fusion | bytes 8388640 | tf_op jit(solution)/shard_map/jit(_take)/gather | solution.py:47
  36.2 6.5 %copy.16 = bf16[8,1024,256]{1,2,0:T(8,128)(2,1)} copy(bf16[8,1024,256]{2,1,0:T(8,128)(2,1)} %bitcast.66) | data formatting | bytes 8388608 | tf_op jit(solution)/shard_map/jit(_take)/gather | solution.py:47
  42.7 6.6 %multiply_reduce_fusion = (f32[8,1024]{1,0:T(8,128)S(1)}, bf16[8,1024,256]{1,2,0:T(8,128)(2,1)S(1)}) fusion(f32[1024,256]{0,1:T(8,128)S(1)} %copy.15, f32[8,1024]{1,0:T(8,128)S(1)} %broadcast_bitcast_fusion, bf16[8,256,256]{2,1,0:T(8,128)(2,1)S(1)} %copy-done, bf16[8,1024,256]{1,2,0:T(8,128)(2,1)} %copy.16, pred[8]{0:T(512)(128)(4,1)S(1)} %get-tuple-element.75), kind=kOutput, calls=%fused_computation.2 | convolution fusion | flops 1103093760 | bytes 10551304 | tf_op jit(solution)/shard_map/epc,ecd->epd/dot_general | solution.py:48
  49.3 2.7 %fusion = f32[8,256,256]{2,1,0:T(8,128)} fusion(bf16[8,1024,256]{1,2,0:T(8,128)(2,1)S(1)} %get-tuple-element.56, bf16[8,1024,256]{1,2,0:T(8,128)(2,1)S(1)} %copy-done.2, pred[8]{0:T(512)(128)(4,1)S(1)} %get-tuple-element.75), kind=kOutput, calls=%fused_computation.7 | convolution fusion | flops 1075838976 | bytes 10485768 | tf_op jit(solution)/shard_map/epc,epd->ecd/dot_general | solution.py:63
  52.0 6.9 %fusion.34 = f32[8,1024,256]{2,1,0:T(8,128)} fusion(bf16[8,1024,256]{1,2,0:T(8,128)(2,1)} %copy-done.1, bf16[8,256,256]{2,1,0:T(8,128)(2,1)S(1)} %copy-done), kind=kOutput, calls=%fused_computation.90 | convolution fusion | flops 1073741824 | bytes 13631488 | tf_op jit(solution)/shard_map/epd,ecd->epc/dot_general | solution.py:66
  58.9 7.9 %gather_fusion.1 = f32[8,8,128,256]{3,2,1,0:T(8,128)} fusion(f32[8,8,128,256]{3,2,1,0:T(8,128)} %bitcast.65, s32[1024]{0:T(1024)S(1)} %pad_clamp_fusion), kind=kCustom, calls=%fused_computation.1 | custom fusion | bytes 16777248 | tf_op jit(solution)/shard_map/jit(_take)/gather | solution.py:70
  66.8 4.4 %broadcast_select_fusion = f32[8,8,128,256]{3,2,1,0:T(8,128)S(1)} fusion(f32[8,8,128,256]{3,2,1,0:T(8,128)} %gather_fusion.1, pred[8]{0:T(512)(128)(4,1)S(1)} %get-tuple-element.76), kind=kLoop, calls=%fused_computation.5 | loop fusion | flops 2097152 | bytes 16777224 | tf_op jit(solution)/shard_map/jit(_take)/select_n | solution.py:70
  71.2 1.0 slice_bitcast_fusion.7
  72.2 1.0 pad_add_fusion
  73.3 3.8 %collective-permute-start.5 = (f32[1,130,256]{2,1,0:T(8,128)S(1)}, f32[1,130,256]{2,1,0:T(8,128)S(1)}, u32[]{:S(2)}, u32[]{:S(2)}) collective-permute-start(f32[1,130,256]{2,1,0:T(8,128)S(1)} %get-tuple-element.68), channel_id=1, source_target_pairs={{4,0},{8,4},{12,8},{0,12},{5,1},{9,5},{13,9},{1,13},{6,2},{10,6},{... | collective-permute-start | bytes 399368 | tf_op jit(solution)/shard_map/ppermute | solution.py:19
  77.2 0.2 fusion.26
  77.4 3.9 %collective-permute-done.4 = f32[1,130,256]{2,1,0:T(8,128)S(1)} collective-permute-done((f32[1,130,256]{2,1,0:T(8,128)S(1)}, f32[1,130,256]{2,1,0:T(8,128)S(1)}, u32[]{:S(2)}, u32[]{:S(2)}) %collective-permute-start.4) | collective-permute-done | bytes 133152 | tf_op jit(solution)/shard_map/ppermute | solution.py:16
  81.3 2.0 %collective-permute-done.5 = f32[1,130,256]{2,1,0:T(8,128)S(1)} collective-permute-done((f32[1,130,256]{2,1,0:T(8,128)S(1)}, f32[1,130,256]{2,1,0:T(8,128)S(1)}, u32[]{:S(2)}, u32[]{:S(2)}) %collective-permute-start.5) | collective-permute-done | bytes 133152 | tf_op jit(solution)/shard_map/ppermute | solution.py:19
  83.3 2.0 %collective-permute-start.7 = (f32[12,1,256]{2,1,0:T(1,128)S(1)}, f32[12,1,256]{2,1,0:T(1,128)S(1)}, u32[]{:S(2)}, u32[]{:S(2)}) collective-permute-start(f32[12,1,256]{2,1,0:T(1,128)S(1)} %get-tuple-element.65), channel_id=1, source_target_pairs={{1,0},{2,1},{3,2},{0,3},{5,4},{6,5},{7,6},{4,7},{9,8},{10,9},{11,1... | collective-permute-start | bytes 36872 | tf_op jit(solution)/shard_map/ppermute | solution.py:19
  85.3 0.7 collective-permute-start.6
  86.0 0.1 pad_maximum_fusion
  86.1 0.1 slice.253
  86.3 2.2 %collective-permute-done.6 = f32[12,1,256]{2,1,0:T(1,128)S(1)} collective-permute-done((f32[12,1,256]{2,1,0:T(1,128)S(1)}, f32[12,1,256]{2,1,0:T(1,128)S(1)}, u32[]{:S(2)}, u32[]{:S(2)}) %collective-permute-start.6) | collective-permute-done | bytes 12320 | tf_op jit(solution)/shard_map/ppermute | solution.py:16
  88.7 1.1 slice.255
  89.8 0.7 fusion.25
  90.4 1.6 fusion.23
  92.0 21.7 %reduce-scatter.2.cloned.1.call-done = f32[128,256]{1,0:T(8,128)} async-done(((f32[2048,256]{1,0:T(8,128)}), f32[128,256]{1,0:T(8,128)}) %reduce-scatter.2.cloned.1.call-update) | async-done | bytes 131088 | tf_op jit(solution)/shard_map/reduce_scatter | solution.py:89
  113.8 1.5 multiply_reduce_fusion.1
  115.3 2.1 %add_convert_fusion = bf16[8,128,256]{2,1,0:T(8,128)(2,1)} fusion(f32[8,128,256]{2,1,0:T(8,128)} %fusion.23, bf16[8,128,256]{2,1,0:T(8,128)(2,1)S(1)} %copy-done.3), kind=kLoop, calls=%fused_computation.20 | loop fusion | flops 786432 | bytes 2097152 | tf_op jit(solution)/shard_map/convert_element_type | solution.py:87
  117.4 30.6 %all-reduce.8 = (f32[]{:T(128)}, f32[32,8]{0,1:T(8,128)S(1)}) all-reduce(f32[]{:T(128)} %multiply_reduce_fusion.1, f32[32,8]{0,1:T(8,128)S(1)} %fusion.26), channel_id=1, replica_groups=mesh['grp'=2,'lat'=4,'lon'=4] {'lat','lon'}, use_global_device_ids=true, to_apply=%region_3.4 | all-reduce | flops 257 | bytes 2056 | tf_op jit(solution)/shard_map/psum | solution.py:90
  148.1 0.6 multiply_reduce_fusion.2
  150.0 0.6 broadcast_multiply_fusion.1
  150.6 1.6 broadcast_multiply_fusion
  (35 shorter events, 0.8 us)
Async XLA Ops:
  7.2 35.5 %copy-start = (bf16[8,256,256]{2,1,0:T(8,128)(2,1)S(1)}, bf16[8,256,256]{2,1,0:T(8,128)(2,1)}, u32[]{:S(2)}) copy-start(bf16[8,256,256]{2,1,0:T(8,128)(2,1)} %param.16) | copy-start | bytes 3145732
  7.2 106.6 %reduce-scatter.2.cloned.1.call-start = ((), (), s32[]{:S(2)}) async-start(), calls=%async_computation.1 | async-start | bytes 2228224 | tf_op jit(solution)/shard_map/reduce_scatter | solution.py:89
  8.2 12.3 %collective-permute-start.1 = (bf16[1,128,256]{2,1,0:T(8,128)(2,1)S(1)}, bf16[1,128,256]{2,1,0:T(8,128)(2,1)S(1)}, u32[]{:S(2)}, u32[]{:S(2)}) collective-permute-start(bf16[1,128,256]{2,1,0:T(8,128)(2,1)S(1)} %get-tuple-element.73), channel_id=1, source_target_pairs={{4,0},{8,4},{12,8},{0,12},{5,1},{9,5},{13,9},{1,13},{6,2},{10,6},{... | collective-permute-start | bytes 196616 | tf_op jit(solution)/shard_map/ppermute | solution.py:19
  13.3 6.1 %collective-permute-start = (bf16[1,128,256]{2,1,0:T(8,128)(2,1)S(1)}, bf16[1,128,256]{2,1,0:T(8,128)(2,1)S(1)}, u32[]{:S(2)}, u32[]{:S(2)}) collective-permute-start(bf16[1,128,256]{2,1,0:T(8,128)(2,1)S(1)} %get-tuple-element.74), channel_id=1, source_target_pairs={{0,4},{4,8},{8,12},{12,0},{1,5},{5,9},{9,13},{13,1},{2,6},{6,10},{... | collective-permute-start | bytes 196616 | tf_op jit(solution)/shard_map/ppermute | solution.py:16
  20.5 3.1 %collective-permute-start.2 = (bf16[10,1,256]{2,1,0:T(2,128)(2,1)S(1)}, bf16[10,1,256]{2,1,0:T(2,128)(2,1)S(1)}, u32[]{:S(2)}, u32[]{:S(2)}) collective-permute-start(bf16[10,1,256]{2,1,0:T(2,128)(2,1)S(1)} %get-tuple-element.71), channel_id=1, source_target_pairs={{0,1},{1,2},{2,3},{3,0},{4,5},{5,6},{6,7},{7,4},{8,9},{9,10},{10,1... | collective-permute-start | bytes 15368 | tf_op jit(solution)/shard_map/ppermute | solution.py:16
  20.6 3.1 %collective-permute-start.3 = (bf16[10,1,256]{2,1,0:T(2,128)(2,1)S(1)}, bf16[10,1,256]{2,1,0:T(2,128)(2,1)S(1)}, u32[]{:S(2)}, u32[]{:S(2)}) collective-permute-start(bf16[10,1,256]{2,1,0:T(2,128)(2,1)S(1)} %get-tuple-element.72), channel_id=1, source_target_pairs={{1,0},{2,1},{3,2},{0,3},{5,4},{6,5},{7,6},{4,7},{9,8},{10,9},{11,1... | collective-permute-start | bytes 15368 | tf_op jit(solution)/shard_map/ppermute | solution.py:19
  42.7 6.7 %copy-start.2 = (bf16[8,1024,256]{1,2,0:T(8,128)(2,1)S(1)}, bf16[8,1024,256]{1,2,0:T(8,128)(2,1)}, u32[]{:S(2)}) copy-start(bf16[8,1024,256]{1,2,0:T(8,128)(2,1)} %copy.16) | copy-start | bytes 12582916
  49.3 2.7 %copy-start.1 = (bf16[8,1024,256]{1,2,0:T(8,128)(2,1)}, bf16[8,1024,256]{1,2,0:T(8,128)(2,1)S(1)}, u32[]{:S(2)}) copy-start(bf16[8,1024,256]{1,2,0:T(8,128)(2,1)S(1)} %get-tuple-element.56) | copy-start | bytes 12582916
  72.2 5.0 %copy-start.4 = (s32[8]{0:T(128)S(1)}, s32[8]{0:T(128)}, u32[]{:S(2)}) copy-start(s32[8]{0:T(128)} %param.18) | copy-start | bytes 100
  73.2 8.1 %collective-permute-start.4 = (f32[1,130,256]{2,1,0:T(8,128)S(1)}, f32[1,130,256]{2,1,0:T(8,128)S(1)}, u32[]{:S(2)}, u32[]{:S(2)}) collective-permute-start(f32[1,130,256]{2,1,0:T(8,128)S(1)} %get-tuple-element.67), channel_id=1, source_target_pairs={{0,4},{4,8},{8,12},{12,0},{1,5},{5,9},{9,13},{13,1},{2,6},{6,10},{... | collective-permute-start | bytes 399368 | tf_op jit(solution)/shard_map/ppermute | solution.py:16
  73.3 10.0 %collective-permute-start.5 = (f32[1,130,256]{2,1,0:T(8,128)S(1)}, f32[1,130,256]{2,1,0:T(8,128)S(1)}, u32[]{:S(2)}, u32[]{:S(2)}) collective-permute-start(f32[1,130,256]{2,1,0:T(8,128)S(1)} %get-tuple-element.68), channel_id=1, source_target_pairs={{4,0},{8,4},{12,8},{0,12},{5,1},{9,5},{13,9},{1,13},{6,2},{10,6},{... | collective-permute-start | bytes 399368 | tf_op jit(solution)/shard_map/ppermute | solution.py:19
  83.3 5.3 %collective-permute-start.7 = (f32[12,1,256]{2,1,0:T(1,128)S(1)}, f32[12,1,256]{2,1,0:T(1,128)S(1)}, u32[]{:S(2)}, u32[]{:S(2)}) collective-permute-start(f32[12,1,256]{2,1,0:T(1,128)S(1)} %get-tuple-element.65), channel_id=1, source_target_pairs={{1,0},{2,1},{3,2},{0,3},{5,4},{6,5},{7,6},{4,7},{9,8},{10,9},{11,1... | collective-permute-start | bytes 36872 | tf_op jit(solution)/shard_map/ppermute | solution.py:19
  85.3 3.1 %collective-permute-start.6 = (f32[12,1,256]{2,1,0:T(1,128)S(1)}, f32[12,1,256]{2,1,0:T(1,128)S(1)}, u32[]{:S(2)}, u32[]{:S(2)}) collective-permute-start(f32[12,1,256]{2,1,0:T(1,128)S(1)} %get-tuple-element.66), channel_id=1, source_target_pairs={{0,1},{1,2},{2,3},{3,0},{4,5},{5,6},{6,7},{7,4},{8,9},{9,10},{10,1... | collective-permute-start | bytes 36872 | tf_op jit(solution)/shard_map/ppermute | solution.py:16
  86.1 29.2 %copy-start.3 = (bf16[8,128,256]{2,1,0:T(8,128)(2,1)S(1)}, bf16[8,128,256]{2,1,0:T(8,128)(2,1)}, u32[]{:S(2)}) copy-start(bf16[8,128,256]{2,1,0:T(8,128)(2,1)} %param.15) | copy-start | bytes 1572868
Sparse Core Ops, SparseCore 0:
  52.2 61.5 reduce-scatter.1
where the time goes:
time: 160 us; the launch traced here: 159 us
  waiting for transfers between devices  32.1 us (20%)
  blocking collectives  30.6 us (19%)
  local copies, waits for them, and re-layouts  25.1 us (16%)
  other arithmetic  24.8 us (16%)
  matrix products  17.3 us (11%)
  between operations  15.6 us (10%)
  starting transfers between devices  13.5 us (8%)
    psum x1, blocking collectives, body(): lax.psum(jnp.sum(weight_shard * weight_shard), ('lat', 'lon'))  30.6 us
    reduce_scatter x1, waiting for transfers between devices, body(): lax.psum_scatter(weight_part, ('lat', 'lon'), scatter_dimension=0, tiled=...  21.7 us
    ppermute x4, starting transfers between devices, with_halo(): lax.ppermute(lax.slice_in_dim(block, 0, width, axis=dim), axis, backward)  12.7 us
    gather x2, local copies, waits for them, and re-layouts, body(): jnp.take(shifted, dir_ids, axis=0)  11.4 us
    ppermute x4, waiting for transfers between devices, with_halo(): lax.ppermute(lax.slice_in_dim(block, block.shape[dim] - width, None, axis...  8.34 us
    gather x1, local copies, waits for them, and re-layouts, body(): by_direction = jnp.take(returned, inverse, axis=0)  7.9 us
    dot_general x1, matrix products, body(): jnp.einsum('epd,ecd->epc', pre_grad, weights, preferred_element_type=jnp....  6.88 us
    dot_general x1, matrix products, body(): jnp.einsum('epc,ecd->epd', neighbours, weights, preferred_element_type=jn...  6.64 us
  transfers between devices with their start and end apart: 9, of which 6 were waited for; matrix products, arithmetic and copies ran while one was open for 20% of the time, Pallas kernels for 0%

commit v1 on v0

--- a/solution.py
+++ b/solution.py
@@ -1,7 +1,356 @@
+import functools
+
 import jax
 import jax.numpy as jnp
 from jax import lax
+from jax.experimental import pallas as pl
+from jax.experimental.pallas import tpu as pltpu
 from jax.sharding import PartitionSpec as P
+
+MESH = pl.DeviceIdType.MESH
+F32, BF16 = jnp.float32, jnp.bfloat16
+DIRS = tuple((a, b) for a in (-1, 0, 1) for b in (-1, 0, 1) if (a, b) != (0, 0))
+
+
+def fused(nlat, nlon, feat, cot, wts, coef, lidx, dirs, gf, gw, gt,
+          P, CT, W, F, S, PG, WG, CR, XS, XR, KP, ZS, ZR, A, T, TR, Q, QR, OH,
+          CS, CV, RS, RV, G,
+          lsem, hs, hr, cs, cr, xs, xr, zs, zr, ts, tr, qs, qr, gs, gr):
+    lat = lax.axis_index("lat")
+    lon = lax.axis_index("lon")
+    size = nlat * nlon
+    me = lat * nlon + lon
+    core = lon % 2
+    side = lon // 2
+    rows, cols, ch = cot.shape
+
+    def rcopy(src, dst, ssem, rsem, to_lat, to_lon):
+        return pltpu.make_async_remote_copy(
+            src_ref=src, dst_ref=dst, send_sem=ssem, recv_sem=rsem,
+            device_id={"lat": to_lat, "lon": to_lon}, device_id_type=MESH)
+
+    loc = [pltpu.make_async_copy(feat, P.at[pl.ds(1, rows), pl.ds(16, cols)], lsem.at[0]),
+           pltpu.make_async_copy(cot, CT, lsem.at[1]),
+           pltpu.make_async_copy(wts, W, lsem.at[2])]
+    for c in loc:
+        c.start()
+
+    barrier = pltpu.get_barrier_semaphore()
+
+    def greet(j, _):
+        o = (me + j) % size
+        pl.semaphore_signal(barrier, inc=1, device_id={"lat": o // nlon, "lon": o % nlon},
+                            device_id_type=MESH)
+        return 0
+    lax.fori_loop(1, size, greet, 0)
+
+    @pl.when(lat == 0)
+    def _():
+        P[0] = jnp.zeros(P.shape[1:], BF16)
+
+    @pl.when(lat == nlat - 1)
+    def _():
+        P[rows + 1] = jnp.zeros(P.shape[1:], BF16)
+
+    lane = lax.broadcasted_iota(jnp.int32, (1, OH.shape[1]), 1)
+    for i in range(rows):
+        OH[i:i + 1, :] = (lane == lidx[i]).astype(F32)
+
+    loc[0].wait()
+    pl.semaphore_wait(barrier, size - 1)
+
+    def halo(m):
+        a, b = DIRS[m]
+        srow = {-1: 1, 0: pl.ds(1, rows), 1: rows}[a]
+        drow = {-1: rows + 1, 0: pl.ds(1, rows), 1: 0}[a]
+        scol = {-1: pl.ds(16, 16), 0: pl.ds(16, cols), 1: pl.ds(cols, 16)}[b]
+        dcol = {-1: pl.ds(16 + cols, 16), 0: pl.ds(16, cols), 1: pl.ds(0, 16)}[b]
+        return rcopy(P.at[srow, scol], P.at[drow, dcol], hs.at[m], hr.at[m],
+                     lat + a, (lon + b + nlon) % nlon)
+
+    def where_ok(pos, fn):
+        pl.when(jnp.logical_and(pos >= 0, pos < nlat))(fn)
+
+    for m, (a, b) in enumerate(DIRS):
+        where_ok(lat + a, lambda m=m: halo(m).start())
+    for m, (a, b) in enumerate(DIRS):
+        where_ok(lat - a, lambda m=m: halo(m).wait_recv())
+
+    for r in range(rows + 2):
+        F[r] = P[r].astype(F32)
+        S[rows + 2 + r] = P[r, 16:16 + cols]
+    for r in range(rows + 2):
+        S[r] = F[r, 15:15 + cols].astype(BF16)
+        S[2 * (rows + 2) + r] = F[r, 17:17 + cols].astype(BF16)
+    loc[1].wait()
+    loc[2].wait()
+
+    def ccopy(i):
+        return rcopy(WG.at[i, 1 - core], CR.at[i], cs.at[i], cr.at[i], lat, lon + 1 - 2 * core)
+
+    def xcopy(s):
+        return rcopy(XS.at[s], XR.at[s], xs.at[s], xr.at[s], lat, (lon + 2) % nlon)
+
+    def zcopy(s):
+        return rcopy(ZS.at[s], ZR.at[s], zs.at[s], zr.at[s], (lat + 1 + s) % nlat, lon)
+
+    def stage_x(s):
+        ccopy(2 * s).wait_recv()
+        ccopy(2 * s + 1).wait_recv()
+        o = 2 * s + 1 - side
+        k = 2 * s + side
+        XS[s] = (WG[o, core] + CR[o]).astype(BF16)
+        xcopy(s).start()
+        KP[s] = WG[k, core] + CR[k]
+
+    def stage_z(s):
+        xcopy(s).wait_recv()
+        ZS[s] = (KP[s] + XR[s].astype(F32)).astype(BF16)
+        zcopy(s).start()
+
+    def step(i, _):
+        s = i // 2
+        e = 2 * ((lat + 1 + s) % nlat) + i % 2
+        k = dirs[e]
+        kp = k + (k >= 4).astype(jnp.int32)
+        base = (kp % 3) * (rows + 2) + kp // 3
+        w = W[e]
+        sums = []
+        for c in range(rows // 2):
+            x = S[pl.ds(base + 2 * c, 2)].reshape(2 * cols, ch)
+            pre2 = jnp.dot(x, w, preferred_element_type=F32)
+            for h in range(2):
+                r = 2 * c + h
+                pre = pre2[h * cols:(h + 1) * cols]
+                sg = 0.5 * jnp.tanh(0.5 * pre) + 0.5
+                act = pre * sg
+                der = sg + act * (1.0 - sg)
+                g = CT[r].astype(F32)
+                sums.append(jnp.sum(g * act, axis=0, keepdims=True))
+                PG[e, r] = (g * coef[lidx[r], e] * der).astype(BF16)
+        wg = lax.dot_general(S[pl.ds(base, rows)].reshape(rows * cols, ch),
+                             PG[e].reshape(rows * cols, ch),
+                             (((0,), (0,)), ((), ())), preferred_element_type=F32)
+        WG[i] = wg.reshape(2, ch // 2, ch)
+        ccopy(i).start()
+        rsum = jnp.sum(jnp.concatenate(sums, axis=0), axis=1, keepdims=True)
+        T[pl.ds(e, 1), :] = jnp.sum(rsum * OH[...], axis=0, keepdims=True)
+
+        @pl.when(jnp.logical_and(i % 2 == 0, i >= 2))
+        def _():
+            stage_x(i // 2 - 1)
+
+        @pl.when(jnp.logical_and(i % 2 == 1, i >= 3))
+        def _():
+            stage_z((i - 3) // 2)
+        return 0
+
+    lax.fori_loop(0, 2 * nlat, step, 0)
+
+    def tcopy(j):
+        o = (me + j) % size
+        return rcopy(T, TR.at[me], ts.at[j], tr.at[j], o // nlon, o % nlon)
+
+    def qcopy(j):
+        o = (me + j) % size
+        return rcopy(Q, QR.at[me], qs.at[j], qr.at[j], o // nlon, o % nlon)
+
+    def each(fn):
+        def run(j, _):
+            fn(j)
+            return 0
+        lax.fori_loop(1, size, run, 0)
+
+    each(lambda j: tcopy(j).start())
+    TR[me] = T[...]
+
+    def expert_of(k):
+        e = jnp.int32(0)
+        for i in range(2 * nlat):
+            e = jnp.where(dirs[i] == k, jnp.int32(i), e)
+        return e
+
+    def back(b):
+        ks = [k for k in range(8) if DIRS[k][1] == b]
+        first = True
+        A[b + 1, 0:1, :, :] = jnp.zeros((1,) + A.shape[2:], F32)
+        A[b + 1, rows + 1:rows + 2, :, :] = jnp.zeros((1,) + A.shape[2:], F32)
+        if b == 0:
+            A[b + 1, rows:rows + 1, :, :] = jnp.zeros((1,) + A.shape[2:], F32)
+        for k in ks:
+            a = DIRS[k][0]
+            e = expert_of(k)
+            ret = lax.dot_general(PG[e].reshape(rows * cols, ch), W[e],
+                                  (((1,), (1,)), ((), ())), preferred_element_type=F32)
+            ret = ret.reshape(rows, cols, ch)
+            if first:
+                A[b + 1, 1 + a:1 + a + rows, 8:8 + cols, :] = ret
+                if b != 0:
+                    A[b + 1, rows:rows + 1, 8:8 + cols, :] = jnp.zeros((1, cols, ch), F32)
+                first = False
+            else:
+                A[b + 1, 1 + a:1 + a + rows, 8:8 + cols, :] += ret
+
+    def colcopy(side_i, a):
+        m = side_i * 3 + a + 1
+        b = 2 * side_i - 1
+        return rcopy(CS.at[side_i], CV.at[m], gs.at[m], gr.at[m],
+                     lat + a, (lon + b + nlon) % nlon)
+
+    def rowcopy(a):
+        m = 6 + (a + 1) // 2
+        return rcopy(RS.at[(a + 1) // 2], RV.at[(a + 1) // 2], gs.at[m], gr.at[m], lat + a, lon)
+
+    back(-1)
+    for r in range(rows + 2):
+        CS[0, r:r + 1, :] = A[0, r, 8:9, :]
+    CS[0, rows + 2:16, :] = jnp.zeros((14 - rows, ch), F32)
+    for a in (-1, 0, 1):
+        where_ok(lat + a, lambda a=a: colcopy(0, a).start())
+    stage_x(nlat - 1)
+    back(1)
+    for r in range(rows + 2):
+        CS[1, r:r + 1, :] = A[2, r, 7 + cols:8 + cols, :]
+    CS[1, rows + 2:16, :] = jnp.zeros((14 - rows, ch), F32)
+    for a in (-1, 0, 1):
+        where_ok(lat + a, lambda a=a: colcopy(1, a).start())
+    back(0)
+    for h, r in ((0, 0), (1, rows + 1)):
+        RS[h] = (A[1, r, 8:8 + cols] + A[0, r, 9:9 + cols] + A[2, r, 7:7 + cols]).astype(BF16)
+    for a in (-1, 1):
+        where_ok(lat + a, lambda a=a: rowcopy(a).start())
+
+    xcopy(nlat - 1).wait_recv()
+    total = KP[nlat - 1] + XR[nlat - 1].astype(F32)
+    for s in range(nlat - 1):
+        zcopy(s).wait_recv()
+        total = total + ZR[s].astype(F32)
+    G[...] = total
+    sq = jnp.sum((total * total).reshape(ch // 16, 8, ch), axis=0)
+    Q[...] = sq[:, :128] + sq[:, 128:]
+    each(lambda j: qcopy(j).start())
+    QR[me] = Q[...]
+
+    for side_i in (0, 1):
+        col = (8 + cols, 7)[side_i]
+        acc = 2 * side_i
+        colcopy(side_i, 0).wait_recv()
+        for i in range(rows):
+            A[acc, 1 + i, col:col + 1, :] = CV[side_i * 3 + 1, 1 + i:2 + i, :]
+
+        def from_below(side_i=side_i, acc=acc, col=col):
+            colcopy(side_i, -1).wait_recv()
+            A[acc, rows, col:col + 1, :] += CV[side_i * 3, 0:1, :]
+
+        def from_above(side_i=side_i, acc=acc, col=col):
+            colcopy(side_i, 1).wait_recv()
+            A[acc, 1, col:col + 1, :] += CV[side_i * 3 + 2, rows + 1:rows + 2, :]
+        where_ok(lat + 1, from_below)
+        where_ok(lat - 1, from_above)
+
+    def row_below():
+        rowcopy(-1).wait_recv()
+        A[1, rows, 8:8 + cols, :] += RV[0].astype(F32)
+
+    def row_above():
+        rowcopy(1).wait_recv()
+        A[1, 1, 8:8 + cols, :] += RV[1].astype(F32)
+    where_ok(lat + 1, row_below)
+    where_ok(lat - 1, row_above)
+    for i in range(rows):
+        gf[i] = (CT[i].astype(F32) + A[1, 1 + i, 8:8 + cols] + A[0, 1 + i, 9:9 + cols]
+                 + A[2, 1 + i, 7:7 + cols]).astype(BF16)
+
+    each(lambda j: tcopy(j).wait_recv())
+    table = TR[0]
+    for j in range(1, size):
+        table = table + TR[j]
+    each(lambda j: qcopy(j).wait_recv())
+    sq = QR[0]
+    for j in range(1, size):
+        sq = sq + QR[j]
+    squares = jnp.sum(sq, keepdims=True) + jnp.sum(table * table, keepdims=True)
+    factor = jnp.minimum(1.0, 512.0 / jnp.sqrt(squares + 1e-06))
+    gw[...] = G[...] * factor
+    scaled = table * factor
+    wide = jnp.concatenate([scaled, jnp.zeros((120, scaled.shape[1]), F32)], axis=0)
+    gt[...] = wide.T[:gt.shape[0], :gt.shape[1]]
+
+    for m, (a, b) in enumerate(DIRS):
+        where_ok(lat + a, lambda m=m: halo(m).wait_send())
+    for i in range(2 * nlat):
+        ccopy(i).wait_send()
+    for s in range(nlat):
+        xcopy(s).wait_send()
+    for s in range(nlat - 1):
+        zcopy(s).wait_send()
+    each(lambda j: tcopy(j).wait_send())
+    each(lambda j: qcopy(j).wait_send())
+    for side_i in (0, 1):
+        for a in (-1, 0, 1):
+            where_ok(lat + a, lambda side_i=side_i, a=a: colcopy(side_i, a).wait_send())
+    for a in (-1, 1):
+        where_ok(lat + a, lambda a=a: rowcopy(a).wait_send())
+
+
+def fused_body(features, cotangent, weights, coef_table, lat_index, dir_ids):
+    nlat, nlon = lax.axis_size("lat"), lax.axis_size("lon")
+    rows, cols, ch = features.shape
+    experts = weights.shape[0]
+    table_rows = coef_table.shape[0]
+    lanes = -(-table_rows // 128) * 128
+    size = nlat * nlon
+    half = ch // 2
+    V = pltpu.VMEM
+    D = pltpu.SemaphoreType.DMA
+    any_spec = pl.BlockSpec(memory_space=pl.ANY)
+    smem = pl.BlockSpec(memory_space=pltpu.SMEM)
+    vmem = pl.BlockSpec(memory_space=pltpu.VMEM)
+    cells = rows * cols
+    return pl.pallas_call(
+        functools.partial(fused, nlat, nlon),
+        out_shape=(jax.ShapeDtypeStruct(features.shape, BF16),
+                   jax.ShapeDtypeStruct((half, ch), F32),
+                   jax.ShapeDtypeStruct((table_rows, experts), F32)),
+        in_specs=[any_spec] * 3 + [smem] * 3,
+        out_specs=(vmem, vmem, vmem),
+        scratch_shapes=[
+            V((rows + 2, cols + 32, ch), BF16),
+            V((rows, cols, ch), BF16),
+            V((experts, ch, ch), BF16),
+            V((rows + 2, cols + 32, ch), F32),
+            V((3 * (rows + 2), cols, ch), BF16),
+            V((experts, rows, cols, ch), BF16),
+            V((experts, 2, half, ch), F32),
+            V((experts, half, ch), F32),
+            V((nlat, half, ch), BF16),
+            V((nlat, half, ch), BF16),
+            V((nlat, half, ch), F32),
+            V((nlat - 1, half, ch), BF16),
+            V((nlat - 1, half, ch), BF16),
+            V((3, rows + 2, cols + 16, ch), F32),
+            V((experts, lanes), F32),
+            V((size, experts, lanes), F32),
+            V((8, 128), F32),
+            V((size, 8, 128), F32),
+            V((rows, lanes), F32),
+            V((2, 16, ch), F32),
+            V((6, 16, ch), F32),
+            V((2, cols, ch), BF16),
+            V((2, cols, ch), BF16),
+            V((half, ch), F32),
+            D((3,)), D((8,)), D((8,)), D((experts,)), D((experts,)),
+            D((nlat,)), D((nlat,)), D((nlat,)), D((nlat,)),
+            D((size,)), D((size,)), D((size,)), D((size,)), D((8,)), D((8,)),
+        ],
+        compiler_params=pltpu.CompilerParams(
+            collective_id=0, has_side_effects=True, vmem_limit_bytes=48 * 1024 * 1024),
+        cost_estimate=pl.CostEstimate(flops=6 * experts * cells * ch * ch,
+                                      bytes_accessed=4 * 1024 * 1024,
+                                      transcendentals=experts * cells * ch),
+        name="relation_backward",
+    )(features, cotangent, weights, coef_table, lat_index, dir_ids)
+
 
 STEP_PAIRS = ((-1, -1), (-1, 0), (-1, 1), (0, -1), (0, 1), (1, -1), (1, 0), (1, 1))
 clip_norm = 512.0
@@ -103,4 +452,6 @@
         P(),
     )
     out_specs = (P(("grp", "lat"), "lon", None), P(("grp", "lat", "lon"), None), P("grp", None))
-    return jax.shard_map(body, mesh=mesh, in_specs=in_specs, out_specs=out_specs, check_vma=False)
+    fits = mesh.shape["lat"] == 4 and mesh.shape["lon"] == 4
+    chosen = fused_body if fits else body
+    return jax.shard_map(chosen, mesh=mesh, in_specs=in_specs, out_specs=out_specs, check_vma=False)

time: 160 us -> 43.3 us (0.27)
  Pallas kernels: 0 us -> 36.2 us
  waiting for transfers between devices: 32.1 us -> 0 us
  blocking collectives: 30.6 us -> 0 us
  other arithmetic: 24.8 us -> 0 us
  local copies, waits for them, and re-layouts: 25.1 us -> 6.19 us
  matrix products: 17.3 us -> 0 us
  between operations: 15.6 us -> 0.67 us
  starting transfers between devices: 13.5 us -> 0 us
    pallas_call x0 -> x1, Pallas kernels: none -> 36.2 us  [fused_body(): pl.pallas_call(functools.partial(fused, nlat, nlon), out_shape=(jax.Shape...]
    psum x1 -> x0, blocking collectives: 30.6 us -> none  [body(): lax.psum(jnp.sum(weight_shard * weight_shard), ('lat', 'lon'))]
    reduce_scatter x1 -> x0, waiting for transfers between devices: 21.7 us -> none  [body(): lax.psum_scatter(weight_part, ('lat', 'lon'), scatter_dimension=0, tiled=...]
    gather x3 -> x0, local copies, waits for them, and re-layouts: 19.3 us -> none  [the longest x2 11.4 us: body(): jnp.take(shifted, dir_ids, axis=0)]
    dot_general x5 -> x0, matrix products: 17.3 us -> none  [the longest x1 6.88 us: body(): jnp.einsum('epd,ecd->epc', pre_grad, weights, preferred_element_type=jnp....]
    ppermute x8 -> x0, starting transfers between devices: 13.5 us -> none  [the longest x4 12.7 us: with_halo(): lax.ppermute(lax.slice_in_dim(block, 0, width, axis=dim), axis, backward)]
    ppermute x8 -> x0, waiting for transfers between devices: 10.4 us -> none  [the longest x4 8.34 us: with_halo(): lax.ppermute(lax.slice_in_dim(block, block.shape[dim] - width, None, axis...]
    unnamed x7 -> x0, other arithmetic: 6.36 us -> none
  transfers between devices with their start and end apart: 9 -> 0, of which waited for: 6 -> 0; matrix products, arithmetic and copies ran while one was open for 20% -> 0% of each run, Pallas kernels for 0% -> 0%
where the time goes in v1:
time: 43.3 us; the launch traced here: 43 us
  Pallas kernels  36.2 us (84%)
  local copies, waits for them, and re-layouts  6.19 us (14%)
  between operations  0.67 us (2%)
    pallas_call x1, Pallas kernels, fused_body(): pl.pallas_call(functools.partial(fused, nlat, nlon), out_shape=(jax.Shape...  36.2 us
    unnamed x13, local copies, waits for them, and re-layouts  5.53 us

profile of v1, /device:TPU:0, one launch (start us, length us, event | category | flops | bytes accessed | tf_op | source)
XLA Modules:
  0.0 43.0 jit_solution(11108060317118978437)
XLA Ops:
  0.6 0.0 copy-start.4
  0.6 0.0 copy-start.3
  0.7 0.8 %copy.9.coef = f32[32,8]{1,0:T(8,128)S(1)} copy(f32[32,8]{0,1:T(8,128)} %param.9) | data formatting | bytes 2048 | tf_op args[3]
  1.4 0.0 copy-done.4
  1.4 0.0 copy-done.3
  1.4 0.0 copy-start
  1.4 1.2 %copy-done = bf16[8,256,256]{2,1,0:T(8,128)(2,1)S(1)} copy-done((bf16[8,256,256]{2,1,0:T(8,128)(2,1)S(1)}, bf16[8,256,256]{2,1,0:T(8,128)(2,1)}, u32[]{:S(2)}) %copy-start) | copy-done | bytes 1048600
  2.7 0.0 copy-start.1
  2.7 1.0 %copy-done.1 = bf16[8,128,256]{2,1,0:T(8,128)(2,1)S(1)} copy-done((bf16[8,128,256]{2,1,0:T(8,128)(2,1)S(1)}, bf16[8,128,256]{2,1,0:T(8,128)(2,1)}, u32[]{:S(2)}) %copy-start.1) | copy-done | bytes 524312
  3.7 0.0 copy-start.2
  3.7 1.0 %copy-done.2 = bf16[8,128,256]{2,1,0:T(8,128)(2,1)S(1)} copy-done((bf16[8,128,256]{2,1,0:T(8,128)(2,1)S(1)}, bf16[8,128,256]{2,1,0:T(8,128)(2,1)}, u32[]{:S(2)}) %copy-start.2) | copy-done | bytes 524312
  4.7 36.2 %relation_backward.1 = (bf16[8,128,256]{2,1,0:T(8,128)(2,1)S(1)}, f32[128,256]{1,0:T(8,128)S(1)}, f32[32,8]{1,0:T(8,128)S(1)}) custom-call(bf16[8,128,256]{2,1,0:T(8,128)(2,1)S(1)} %copy-done.1, bf16[8,128,256]{2,1,0:T(8,128)(2,1)S(1)} %copy-done.2, bf16[8,256,256]{2,1,0:T(8,128)(2,1)S(1)} %copy-done, f32[32,8]{1,0:T(8,128)S(1)} %copy.9.coef, ...), custom_call_target="tpu_custom_call" | custom-call | flops 3221225472 | bytes 4194304 | tf_op jit(solution)/shard_map/relation_backward/pallas_call | solution.py:310
  40.9 0.7 %copy.10 = f32[32,8]{0,1:T(8,128)} copy(f32[32,8]{1,0:T(8,128)S(1)} %get-tuple-element.5) | data formatting | bytes 2048 | tf_op jit(solution)/shard_map/relation_backward/pallas_call | solution.py:310
  41.6 0.8 %copy.13 = bf16[8,128,256]{2,1,0:T(8,128)(2,1)} copy(bf16[8,128,256]{2,1,0:T(8,128)(2,1)S(1)} %get-tuple-element.9) | data formatting | bytes 1048576
  42.4 0.7 %copy.14 = f32[128,256]{1,0:T(8,128)} copy(f32[128,256]{1,0:T(8,128)S(1)} %get-tuple-element.10) | data formatting | bytes 262144
Async XLA Ops:
  0.6 0.8 %copy-start.4 = (s32[8]{0:T(128)S(1)}, s32[8]{0:T(128)}, u32[]{:S(2)}) copy-start(s32[8]{0:T(128)} %dirs.1) | copy-start | bytes 100
  0.6 0.8 %copy-start.3 = (s32[8]{0:T(128)S(1)}, s32[8]{0:T(128)}, u32[]{:S(2)}) copy-start(s32[8]{0:T(128)} %lidx.1) | copy-start | bytes 100
  1.4 1.2 %copy-start = (bf16[8,256,256]{2,1,0:T(8,128)(2,1)S(1)}, bf16[8,256,256]{2,1,0:T(8,128)(2,1)}, u32[]{:S(2)}) copy-start(bf16[8,256,256]{2,1,0:T(8,128)(2,1)} %wts.1) | copy-start | bytes 3145732
  2.7 1.0 %copy-start.1 = (bf16[8,128,256]{2,1,0:T(8,128)(2,1)S(1)}, bf16[8,128,256]{2,1,0:T(8,128)(2,1)}, u32[]{:S(2)}) copy-start(bf16[8,128,256]{2,1,0:T(8,128)(2,1)} %feat.1) | copy-start | bytes 1572868
  3.7 1.0 %copy-start.2 = (bf16[8,128,256]{2,1,0:T(8,128)(2,1)S(1)}, bf16[8,128,256]{2,1,0:T(8,128)(2,1)}, u32[]{:S(2)}) copy-start(bf16[8,128,256]{2,1,0:T(8,128)(2,1)} %cot.1) | copy-start | bytes 1572868

commit v2 on v1

--- a/solution.py
+++ b/solution.py
@@ -127,7 +127,7 @@
                 der = sg + act * (1.0 - sg)
                 g = CT[r].astype(F32)
                 sums.append(jnp.sum(g * act, axis=0, keepdims=True))
-                PG[e, r] = (g * coef[lidx[r], e] * der).astype(BF16)
+                PG[e, r] = (g * coef[e, lidx[r]] * der).astype(BF16)
         wg = lax.dot_general(S[pl.ds(base, rows)].reshape(rows * cols, ch),
                              PG[e].reshape(rows * cols, ch),
                              (((0,), (0,)), ((), ())), preferred_element_type=F32)
@@ -140,9 +140,9 @@
         def _():
             stage_x(i // 2 - 1)
 
-        @pl.when(jnp.logical_and(i % 2 == 1, i >= 3))
+        @pl.when(jnp.logical_and(i % 2 == 1, i >= 5))
         def _():
-            stage_z((i - 3) // 2)
+            stage_z((i - 5) // 2)
         return 0
 
     lax.fori_loop(0, 2 * nlat, step, 0)
@@ -214,6 +214,7 @@
     CS[1, rows + 2:16, :] = jnp.zeros((14 - rows, ch), F32)
     for a in (-1, 0, 1):
         where_ok(lat + a, lambda a=a: colcopy(1, a).start())
+    stage_z(nlat - 2)
     back(0)
     for h, r in ((0, 0), (1, rows + 1)):
         RS[h] = (A[1, r, 8:8 + cols] + A[0, r, 9:9 + cols] + A[2, r, 7:7 + cols]).astype(BF16)
@@ -273,8 +274,7 @@
     factor = jnp.minimum(1.0, 512.0 / jnp.sqrt(squares + 1e-06))
     gw[...] = G[...] * factor
     scaled = table * factor
-    wide = jnp.concatenate([scaled, jnp.zeros((120, scaled.shape[1]), F32)], axis=0)
-    gt[...] = wide.T[:gt.shape[0], :gt.shape[1]]
+    gt[...] = scaled[:, :gt.shape[1]]
 
     for m, (a, b) in enumerate(DIRS):
         where_ok(lat + a, lambda m=m: halo(m).wait_send())
@@ -307,11 +307,11 @@
     smem = pl.BlockSpec(memory_space=pltpu.SMEM)
     vmem = pl.BlockSpec(memory_space=pltpu.VMEM)
     cells = rows * cols
-    return pl.pallas_call(
+    grad_features, grad_weights, grad_table = pl.pallas_call(
         functools.partial(fused, nlat, nlon),
         out_shape=(jax.ShapeDtypeStruct(features.shape, BF16),
                    jax.ShapeDtypeStruct((half, ch), F32),
-                   jax.ShapeDtypeStruct((table_rows, experts), F32)),
+                   jax.ShapeDtypeStruct((experts, table_rows), F32)),
         in_specs=[any_spec] * 3 + [smem] * 3,
         out_specs=(vmem, vmem, vmem),
         scratch_shapes=[
@@ -344,12 +344,13 @@
             D((size,)), D((size,)), D((size,)), D((size,)), D((8,)), D((8,)),
         ],
         compiler_params=pltpu.CompilerParams(
-            collective_id=0, has_side_effects=True, vmem_limit_bytes=48 * 1024 * 1024),
+            collective_id=0, has_side_effects=True, vmem_limit_bytes=62 * 1024 * 1024),
         cost_estimate=pl.CostEstimate(flops=6 * experts * cells * ch * ch,
                                       bytes_accessed=4 * 1024 * 1024,
                                       transcendentals=experts * cells * ch),
         name="relation_backward",
-    )(features, cotangent, weights, coef_table, lat_index, dir_ids)
+    )(features, cotangent, weights, coef_table.T, lat_index, dir_ids)
+    return grad_features, grad_weights, grad_table.T
 
 
 STEP_PAIRS = ((-1, -1), (-1, 0), (-1, 1), (0, -1), (0, 1), (1, -1), (1, 0), (1, 1))

time: 43.3 us -> 36.8 us (0.85)
  Pallas kernels: 36.2 us -> 32.8 us
  local copies, waits for them, and re-layouts: 6.19 us -> 3.18 us
    pallas_call x1, Pallas kernels: 36.2 us -> 32.8 us  [fused_body(): pl.pallas_call(functools.partial(fused, nlat, nlon), out_shape=(jax.Shape...]
    unnamed x13 -> x7, local copies, waits for them, and re-layouts: 5.53 us -> 3.18 us
    pallas_call x1 -> x0, local copies, waits for them, and re-layouts: 0.66 us -> none  [fused_body(): pl.pallas_call(functools.partial(fused, nlat, nlon), out_shape=(jax.Shape...]
where the time goes in v2:
time: 36.8 us; the launch traced here: 36.6 us
  Pallas kernels  32.8 us (89%)
  local copies, waits for them, and re-layouts  3.18 us (9%)
  between operations  0.65 us (2%)
    pallas_call x1, Pallas kernels, fused_body(): pl.pallas_call(functools.partial(fused, nlat, nlon), out_shape=(jax.Shape...  32.8 us
    unnamed x7, local copies, waits for them, and re-layouts  3.18 us

profile of v2, /device:TPU:0, one launch (start us, length us, event | category | flops | bytes accessed | tf_op | source)
XLA Modules:
  0.0 36.6 jit_solution(13648799578913474109)
XLA Ops:
  0.6 32.8 %relation_backward.1 = (bf16[8,128,256]{2,1,0:T(8,128)(2,1)}, f32[128,256]{1,0:T(8,128)}, f32[8,32]{1,0:T(8,128)}) custom-call(bf16[8,128,256]{2,1,0:T(8,128)(2,1)} %feat.1, bf16[8,128,256]{2,1,0:T(8,128)(2,1)} %cot.1, bf16[8,256,256]{2,1,0:T(8,128)(2,1)} %wts.1, f32[8,32]{1,0:T(8,128)} %bitcast.3, s32[8]{0:T(128)} %lidx.1, s32[8]{0:T(128)} %dirs.1), custom_call_target="tpu_custom_call" | custom-call | flops 3221225472 | bytes 4194304 | tf_op jit(solution)/shard_map/relation_backward/pallas_call | solution.py:310
  33.4 0.0 copy-start
  33.4 1.9 %copy.12 = bf16[8,128,256]{2,1,0:T(8,128)(2,1)} copy(bf16[8,128,256]{2,1,0:T(8,128)(2,1)} %get-tuple-element.12) | data formatting | bytes 1048576
  35.3 0.0 copy-done
  35.3 0.0 copy-start.1
  35.3 0.7 %copy.13 = f32[128,256]{1,0:T(8,128)} copy(f32[128,256]{1,0:T(8,128)S(1)} %copy-done) | data formatting | bytes 262144
  36.0 0.0 copy-done.1
  36.0 0.6 %copy.14 = f32[32,8]{0,1:T(8,128)} copy(f32[32,8]{0,1:T(8,128)S(1)} %bitcast.2) | data formatting | bytes 2048
Async XLA Ops:
  33.4 1.9 %copy-start = (f32[128,256]{1,0:T(8,128)S(1)}, f32[128,256]{1,0:T(8,128)}, u32[]{:S(2)}) copy-start(f32[128,256]{1,0:T(8,128)} %get-tuple-element.13) | copy-start | bytes 393220
  35.3 0.7 %copy-start.1 = (f32[8,32]{1,0:T(8,128)S(1)}, f32[8,32]{1,0:T(8,128)}, u32[]{:S(2)}) copy-start(f32[8,32]{1,0:T(8,128)} %get-tuple-element.8) | copy-start | bytes 3076

commit v3 on v2

--- a/solution.py
+++ b/solution.py
@@ -15,7 +15,7 @@
 def fused(nlat, nlon, feat, cot, wts, coef, lidx, dirs, gf, gw, gt,
           P, CT, W, F, S, PG, WG, CR, XS, XR, KP, ZS, ZR, A, T, TR, Q, QR, OH,
           CS, CV, RS, RV, G,
-          lsem, hs, hr, cs, cr, xs, xr, zs, zr, ts, tr, qs, qr, gs, gr):
+          GF, lsem, hs, hr, cs, cr, xs, xr, zs, zr, ts, tr, qs, qr, gs, gr):
     lat = lax.axis_index("lat")
     lon = lax.axis_index("lon")
     size = nlat * nlon
@@ -73,15 +73,27 @@
 
     for m, (a, b) in enumerate(DIRS):
         where_ok(lat + a, lambda m=m: halo(m).start())
+    n = rows + 2
+    for r in range(1, rows + 1):
+        F[r, 16:16 + cols] = P[r, 16:16 + cols].astype(F32)
+        S[n + r] = P[r, 16:16 + cols]
+    for r in range(1, rows + 1):
+        S[r, 16:cols] = F[r, 31:15 + cols].astype(BF16)
+        S[2 * n + r, 0:cols - 16] = F[r, 17:1 + cols].astype(BF16)
     for m, (a, b) in enumerate(DIRS):
         where_ok(lat - a, lambda m=m: halo(m).wait_recv())
-
-    for r in range(rows + 2):
+    for r in range(1, rows + 1):
+        F[r, 0:16] = P[r, 0:16].astype(F32)
+        F[r, 16 + cols:] = P[r, 16 + cols:].astype(F32)
+    for r in (0, rows + 1):
         F[r] = P[r].astype(F32)
-        S[rows + 2 + r] = P[r, 16:16 + cols]
-    for r in range(rows + 2):
+        S[n + r] = P[r, 16:16 + cols]
+    for r in range(1, rows + 1):
+        S[r, 0:16] = F[r, 15:31].astype(BF16)
+        S[2 * n + r, cols - 16:cols] = F[r, 1 + cols:17 + cols].astype(BF16)
+    for r in (0, rows + 1):
         S[r] = F[r, 15:15 + cols].astype(BF16)
-        S[2 * (rows + 2) + r] = F[r, 17:17 + cols].astype(BF16)
+        S[2 * n + r] = F[r, 17:17 + cols].astype(BF16)
     loc[1].wait()
     loc[2].wait()
 
@@ -114,7 +126,7 @@
         k = dirs[e]
         kp = k + (k >= 4).astype(jnp.int32)
         base = (kp % 3) * (rows + 2) + kp // 3
-        w = W[e]
+        w = W[e] * jnp.asarray(0.5, BF16)
         sums = []
         for c in range(rows // 2):
             x = S[pl.ds(base + 2 * c, 2)].reshape(2 * cols, ch)
@@ -122,12 +134,13 @@
             for h in range(2):
                 r = 2 * c + h
                 pre = pre2[h * cols:(h + 1) * cols]
-                sg = 0.5 * jnp.tanh(0.5 * pre) + 0.5
-                act = pre * sg
-                der = sg + act * (1.0 - sg)
+                th = jnp.tanh(pre)
+                up = 1.0 + th
+                act = pre * up
+                der = up + act * (1.0 - th)
                 g = CT[r].astype(F32)
                 sums.append(jnp.sum(g * act, axis=0, keepdims=True))
-                PG[e, r] = (g * coef[e, lidx[r]] * der).astype(BF16)
+                PG[e, r] = (g * (0.5 * coef[e, lidx[r]]) * der).astype(BF16)
         wg = lax.dot_general(S[pl.ds(base, rows)].reshape(rows * cols, ch),
                              PG[e].reshape(rows * cols, ch),
                              (((0,), (0,)), ((), ())), preferred_element_type=F32)
@@ -160,9 +173,6 @@
             fn(j)
             return 0
         lax.fori_loop(1, size, run, 0)
-
-    each(lambda j: tcopy(j).start())
-    TR[me] = T[...]
 
     def expert_of(k):
         e = jnp.int32(0)
@@ -202,19 +212,21 @@
         return rcopy(RS.at[(a + 1) // 2], RV.at[(a + 1) // 2], gs.at[m], gr.at[m], lat + a, lon)
 
     back(-1)
+    stage_x(nlat - 1)
+    stage_z(nlat - 2)
     for r in range(rows + 2):
         CS[0, r:r + 1, :] = A[0, r, 8:9, :]
     CS[0, rows + 2:16, :] = jnp.zeros((14 - rows, ch), F32)
     for a in (-1, 0, 1):
         where_ok(lat + a, lambda a=a: colcopy(0, a).start())
-    stage_x(nlat - 1)
+    each(lambda j: tcopy(j).start())
+    TR[me] = T[...]
     back(1)
     for r in range(rows + 2):
         CS[1, r:r + 1, :] = A[2, r, 7 + cols:8 + cols, :]
     CS[1, rows + 2:16, :] = jnp.zeros((14 - rows, ch), F32)
     for a in (-1, 0, 1):
         where_ok(lat + a, lambda a=a: colcopy(1, a).start())
-    stage_z(nlat - 2)
     back(0)
     for h, r in ((0, 0), (1, rows + 1)):
         RS[h] = (A[1, r, 8:8 + cols] + A[0, r, 9:9 + cols] + A[2, r, 7:7 + cols]).astype(BF16)
@@ -259,8 +271,10 @@
     where_ok(lat + 1, row_below)
     where_ok(lat - 1, row_above)
     for i in range(rows):
-        gf[i] = (CT[i].astype(F32) + A[1, 1 + i, 8:8 + cols] + A[0, 1 + i, 9:9 + cols]
+        GF[i] = (CT[i].astype(F32) + A[1, 1 + i, 8:8 + cols] + A[0, 1 + i, 9:9 + cols]
                  + A[2, 1 + i, 7:7 + cols]).astype(BF16)
+    out = pltpu.make_async_copy(GF, gf, lsem.at[3])
+    out.start()
 
     each(lambda j: tcopy(j).wait_recv())
     table = TR[0]
@@ -276,6 +290,7 @@
     scaled = table * factor
     gt[...] = scaled[:, :gt.shape[1]]
 
+    out.wait()
     for m, (a, b) in enumerate(DIRS):
         where_ok(lat + a, lambda m=m: halo(m).wait_send())
     for i in range(2 * nlat):
@@ -293,6 +308,12 @@
         where_ok(lat + a, lambda a=a: rowcopy(a).wait_send())
 
 
+def place(a, b, c, x, y, z):
+    x[...] = a[...]
+    y[...] = b[...]
+    z[...] = c[...]
+
+
 def fused_body(features, cotangent, weights, coef_table, lat_index, dir_ids):
     nlat, nlon = lax.axis_size("lat"), lax.axis_size("lon")
     rows, cols, ch = features.shape
@@ -307,13 +328,13 @@
     smem = pl.BlockSpec(memory_space=pltpu.SMEM)
     vmem = pl.BlockSpec(memory_space=pltpu.VMEM)
     cells = rows * cols
-    grad_features, grad_weights, grad_table = pl.pallas_call(
+    found = pl.pallas_call(
         functools.partial(fused, nlat, nlon),
         out_shape=(jax.ShapeDtypeStruct(features.shape, BF16),
                    jax.ShapeDtypeStruct((half, ch), F32),
                    jax.ShapeDtypeStruct((experts, table_rows), F32)),
         in_specs=[any_spec] * 3 + [smem] * 3,
-        out_specs=(vmem, vmem, vmem),
+        out_specs=(any_spec, vmem, vmem),
         scratch_shapes=[
             V((rows + 2, cols + 32, ch), BF16),
             V((rows, cols, ch), BF16),
@@ -339,7 +360,8 @@
             V((2, cols, ch), BF16),
             V((2, cols, ch), BF16),
             V((half, ch), F32),
-            D((3,)), D((8,)), D((8,)), D((experts,)), D((experts,)),
+            V((rows, cols, ch), BF16),
+            D((4,)), D((8,)), D((8,)), D((experts,)), D((experts,)),
             D((nlat,)), D((nlat,)), D((nlat,)), D((nlat,)),
             D((size,)), D((size,)), D((size,)), D((size,)), D((8,)), D((8,)),
         ],
@@ -350,6 +372,14 @@
                                       transcendentals=experts * cells * ch),
         name="relation_backward",
     )(features, cotangent, weights, coef_table.T, lat_index, dir_ids)
+    grad_features, grad_weights, grad_table = pl.pallas_call(
+        place,
+        out_shape=[jax.ShapeDtypeStruct(x.shape, x.dtype) for x in found],
+        in_specs=[vmem] * 3,
+        out_specs=[vmem] * 3,
+        compiler_params=pltpu.CompilerParams(vmem_limit_bytes=62 * 1024 * 1024),
+        name="place_results",
+    )(*found)
     return grad_features, grad_weights, grad_table.T
 
 

time: 36.8 us -> 34.6 us (0.940)
  local copies, waits for them, and re-layouts: 3.18 us -> 0 us
  Pallas kernels: 32.8 us -> 33.8 us
    unnamed x7 -> x0, local copies, waits for them, and re-layouts: 3.18 us -> none
    pallas_call x0 -> x1, Pallas kernels: none -> 1.97 us  [fused_body(): pl.pallas_call(place, out_shape=[jax.ShapeDtypeStruct(x.shape, x.dtype) f...]
    pallas_call x1, Pallas kernels: 32.8 us -> 31.8 us  [fused_body(): pl.pallas_call(functools.partial(fused, nlat, nlon), out_shape=(jax.Shape...]
where the time goes in v3:
time: 34.6 us; the launch traced here: 34.4 us
  Pallas kernels  33.8 us (98%)
  between operations  0.64 us (2%)
    pallas_call x1, Pallas kernels, fused_body(): pl.pallas_call(functools.partial(fused, nlat, nlon), out_shape=(jax.Shape...  31.8 us
    pallas_call x1, Pallas kernels, fused_body(): pl.pallas_call(place, out_shape=[jax.ShapeDtypeStruct(x.shape, x.dtype) f...  1.97 us

profile of v3, /device:TPU:0, one launch (start us, length us, event | category | flops | bytes accessed | tf_op | source)
XLA Modules:
  0.0 34.4 jit_solution(4519993471993000394)
XLA Ops:
  0.6 31.8 %relation_backward.1 = (bf16[8,128,256]{2,1,0:T(8,128)(2,1)}, f32[128,256]{1,0:T(8,128)}, f32[8,32]{1,0:T(8,128)}) custom-call(bf16[8,128,256]{2,1,0:T(8,128)(2,1)} %feat.1, bf16[8,128,256]{2,1,0:T(8,128)(2,1)} %cot.1, bf16[8,256,256]{2,1,0:T(8,128)(2,1)} %wts.1, f32[8,32]{1,0:T(8,128)} %bitcast.2, s32[8]{0:T(128)} %lidx.1, s32[8]{0:T(128)} %dirs.1), custom_call_target="tpu_custom_call" | custom-call | flops 3221225472 | bytes 4194304 | tf_op jit(solution)/shard_map/relation_backward/pallas_call | solution.py:331
  32.4 2.0 %place_results.1 = (bf16[8,128,256]{2,1,0:T(8,128)(2,1)}, f32[128,256]{1,0:T(8,128)}, f32[8,32]{1,0:T(8,128)}) custom-call(bf16[8,128,256]{2,1,0:T(8,128)(2,1)} %get-tuple-element.9.a, f32[128,256]{1,0:T(8,128)} %get-tuple-element.10.b, f32[8,32]{1,0:T(8,128)} %get-tuple-element.11.c), custom_call_target="tpu_custom_call" | custom-call | tf_op jit(solution)/shard_map/place_results/pallas_call | solution.py:375
